TPU v7x, 32 devices: a whole 2x2x4 slice. The times are simulated.
32 devices in a mesh: rep: 2 (over y), dec: 4 (over z), tp: 4 (over x, core).
Axes of the slice: x: 2, y: 2, z: 4, core: 2. Of those that a mesh axis runs over, the one named last changes fastest.
Arguments:
- token_states: bfloat16 [64, 2, 5120], P(('rep', 'dec')), parts along dimension 0, may hold values from -6 to 6
- query_rows: bfloat16 [64, 2, 4096], P(('rep', 'dec'), None, 'tp'), parts along dimension 0, may hold values from -400 to 400
- key_weight: bfloat16 [5120, 512], P(None, 'tp'), may hold values from -0.078125 to 0.078125
- value_weight: bfloat16 [5120, 512], P(None, 'tp'), may hold values from -0.078125 to 0.078125
- out_weight: bfloat16 [4096, 2560], P('tp'), may hold values from -0.5 to 0.5
- key_pool: bfloat16 [256, 4, 128, 128], P(('rep', 'dec'), 'tp'), parts along dimension 0, may hold values from -6 to 6
- value_pool: bfloat16 [256, 4, 128, 128], P(('rep', 'dec'), 'tp'), parts along dimension 0, may hold values from -6 to 6
- cached_len: int32 [8, 8], P('rep'), parts along dimension 0, may hold values from 0 to 510, as said below
- page_table: int32 [8, 8, 4], P(('rep', 'dec')), parts along dimension 0, may hold values from 0 to 31, as said below
- migrations: int32 [8, 4], P('rep'), parts along dimension 0, may hold values from 0 to 7, as said below
Outputs:
- mixed: bfloat16 [64, 2, 2560], P(('rep', 'dec')), parts along dimension 0
- key_pool_out: bfloat16 [256, 4, 128, 128], P(('rep', 'dec'), 'tp'), parts along dimension 0
- value_pool_out: bfloat16 [256, 4, 128, 128], P(('rep', 'dec'), 'tp'), parts along dimension 0
There are 2 independent parts, one for each index of `rep`. A program takes and returns all parts, laid end to end along the dimension named above; an argument that names none is the same for every part. Nothing has to cross between parts.
Inputs may be any that keep to these rules, and one draw needn't show every extreme that they name: `migrations`: the groups form pairs g and g + 2; in each pair one group sends and the other receives. The sender of pair i sends one response from each of 2 distinct slots, to the receivers of pairs i and i + 1 (mod 2); every receiver gets 2 responses into distinct slots. Rows are in any order. `cached_len`: 0 exactly for the slots that receive a response; sending groups' slots hold 255 or more tokens, receiving groups' other slots 128 or fewer; in every draw at least one moving response has exactly 510 tokens. `page_table`: each group's table names every page 0 to 31 of its pool once.
All inputs are finite; a program needn't handle non-finite values.
Results may differ from a plain program's by a relative error of at most 0.0059.
Values may be sent and summed in bfloat16 or wider, within the bound.
No kernel may reach another device: no remote copies, remote signals or barrier semaphores. Data moves between devices by JAX's collectives and lax.ppermute only.
A program may use at most 64 MiB of HBM per device.

v0:
```python
import functools

import jax
import jax.numpy as jnp
from jax import lax
from jax.experimental import pallas as pl
from jax.experimental.pallas import tpu as pltpu
from jax.sharding import PartitionSpec as P

F32 = jnp.float32
BF16 = jnp.bfloat16
PARTS = 4
SMEM = pl.BlockSpec(memory_space=pltpu.SMEM)
HBM = pl.BlockSpec(memory_space=pltpu.HBM)
ANY = pl.BlockSpec(memory_space=pl.ANY)
VMEM = pl.BlockSpec(memory_space=pltpu.VMEM)


def shifted(count, by):
    return [(i, (i + by) % count) for i in range(count)]


def outgoing(mig, me, groups):
    half = groups // 2
    near = far = jnp.int32(-1)
    for m in range(mig.shape[0]):
        mine = mig[m, 0] == me
        gap = lax.rem(mig[m, 2] - me + groups, groups)
        near = jnp.where(mine & (gap == half), mig[m, 1], near)
        far = jnp.where(mine & (gap != half), mig[m, 1], far)
    return near, far


def incoming(mig, lens, me, groups):
    half = groups // 2
    near = far = jnp.int32(-1)
    near_len = far_len = far_gap = jnp.int32(0)
    for m in range(mig.shape[0]):
        mine = mig[m, 2] == me
        gap = lax.rem(me - mig[m, 0] + groups, groups)
        length = lens[mig[m, 0], mig[m, 1]]
        is_near = mine & (gap == half)
        is_far = mine & (gap != half)
        near = jnp.where(is_near, mig[m, 3], near)
        near_len = jnp.where(is_near, length, near_len)
        far = jnp.where(is_far, mig[m, 3], far)
        far_len = jnp.where(is_far, length, far_len)
        far_gap = jnp.where(is_far, gap, far_gap)
    return (near, near_len), (far, far_len), far_gap


def pack_kernel(groups, mig, table, key_pool, value_pool, near_out, far_out, token, sems):
    me = lax.axis_index("dec")
    pages = table.shape[1]
    outs = (near_out, far_out)
    slots = outgoing(mig, me, groups)

    def load(n, which, p):
        page = table[0, p, slots[n]]
        pool = (key_pool, value_pool)[which]
        return pltpu.make_async_copy(pool.at[page], outs[n].at[which * pages + p], sems.at[n, which, p])

    def each(do):
        for n in range(2):

            @pl.when(slots[n] >= 0)
            def _():
                for p in range(pages):
                    for which in range(2):
                        do(load(n, which, p))

    each(lambda copy: copy.start())
    token[0] = me
    each(lambda copy: copy.wait())


def attend_kernel(
    groups,
    token,
    mig,
    lens,
    table,
    states,
    query,
    key_weight,
    value_weight,
    out_weight,
    key_pool,
    value_pool,
    key_out,
    value_out,
    partial,
    new_rows,
    wk,
    wv,
    wo,
    kp,
    vp,
    q_scr,
    a_scr,
    n_scr,
    sems,
):
    del token
    me = lax.axis_index("dec")
    slot_count, steps, _ = states.shape
    rows = slot_count * steps
    pages = table.shape[1]
    page_len, head_dim = kp.shape[1:]
    heads = query.shape[2] // head_dim
    span = pages * page_len
    number = 0

    def split(source, target, parts):
        nonlocal number
        size = source.shape[0] // parts
        copies = []
        for part in range(parts):
            piece = pl.ds(part * size, size)
            copies.append(pltpu.make_async_copy(source.at[piece], target.at[piece], sems.at[number]))
            number += 1
        return copies

    load_keys = split(key_pool, kp, PARTS)
    load_wk = split(key_weight, wk, PARTS)
    load_wv = split(value_weight, wv, PARTS)
    load_values = split(value_pool, vp, PARTS)
    load_wo = split(out_weight, wo, PARTS)
    for load in load_keys + load_wk + load_wv + load_values + load_wo:
        load.start()
    near, far = outgoing(mig, me, groups)
    lengths = [lens[me, s] for s in range(slot_count)]

    for s in range(slot_count):
        qf = query[s].astype(F32)
        for h in range(heads):
            q_scr[pl.ds(h * rows + s * steps, steps), :] = qf[:, h * head_dim : (h + 1) * head_dim]
    x = jnp.concatenate([states[s].astype(F32) for s in range(slot_count)], 0).astype(BF16)
    queries = [
        jnp.concatenate(
            [q_scr[pl.ds(s * steps + t, heads, stride=rows), :] for t in range(steps)], 0
        ).astype(BF16)
        for s in range(slot_count)
    ]

    scaling = head_dim**-0.5
    count = steps * heads
    fresh_col = lax.broadcasted_iota(jnp.int32, (count, rows), 1)
    fresh_step = lax.broadcasted_iota(jnp.int32, (count, rows), 0) // heads
    position = lax.broadcasted_iota(jnp.int32, (count, span), 1)
    nt = (((1,), (1,)), ((), ()))
    numbers = [[table[0, p, s] for p in range(pages)] for s in range(slot_count)]
    for load in load_keys:
        load.wait()
    scores = []
    for s in range(slot_count):
        keys = jnp.concatenate([kp[n] for n in numbers[s]], 0)
        cached = lax.dot_general(queries[s], keys, nt, preferred_element_type=F32) * scaling
        scores.append(jnp.where(position < lengths[s], cached, -jnp.inf))

    fresh_k = jnp.zeros((rows, head_dim), F32)
    fresh_v = jnp.zeros((rows, head_dim), F32)
    size = wk.shape[0] // PARTS
    for part in range(PARTS):
        piece = slice(part * size, (part + 1) * size)
        load_wk[part].wait()
        fresh_k = fresh_k + jnp.dot(x[:, piece], wk[piece, :], preferred_element_type=F32)
        load_wv[part].wait()
        fresh_v = fresh_v + jnp.dot(x[:, piece], wv[piece, :], preferred_element_type=F32)
    fresh_rows = jnp.concatenate([fresh_k, fresh_v], 1).astype(BF16)
    new_rows[...] = fresh_rows
    n_scr[...] = fresh_rows.astype(F32)
    new_k = fresh_rows[:, :head_dim]
    new_v = fresh_rows[:, head_dim:]

    for load in load_values:
        load.wait()
    for s in range(slot_count):
        values = jnp.concatenate([vp[n] for n in numbers[s]], 0)
        cached = scores[s]
        fresh = lax.dot_general(queries[s], new_k, nt, preferred_element_type=F32) * scaling
        ok = (fresh_col >= s * steps) & (fresh_col <= s * steps + fresh_step)
        fresh = jnp.where(ok, fresh, -jnp.inf)
        peak = jnp.maximum(jnp.max(cached, 1, keepdims=True), jnp.max(fresh, 1, keepdims=True))
        cached = jnp.exp(cached - peak)
        fresh = jnp.exp(fresh - peak)
        total = jnp.sum(cached, 1, keepdims=True) + jnp.sum(fresh, 1, keepdims=True)
        cached_w = (cached / total).astype(BF16)
        fresh_w = (fresh / total).astype(BF16)
        out = jnp.dot(cached_w, values, preferred_element_type=F32)
        out = out + jnp.dot(fresh_w, new_v, preferred_element_type=F32)
        for t in range(steps):
            a_scr[pl.ds(s * steps + t, heads, stride=rows), :] = out[t * heads : (t + 1) * heads]

    tile = 16
    row = lax.broadcasted_iota(jnp.int32, (tile, head_dim), 0)
    tiles = []
    for s in range(slot_count):
        live = (lengths[s] > 0) & (s != near) & (s != far)
        first = jnp.where(live, lengths[s], -steps)
        for t in range(steps):
            at = lengths[s] + t
            page = table[0, at // page_len, s]
            low = at // tile * tile
            base = pl.multiple_of(lax.rem(low, page_len), tile)
            for pool, side in ((kp, 0), (vp, head_dim)):
                merged = pool[page, pl.ds(base, tile), :].astype(F32)
                for u in range(steps):
                    fresh_row = n_scr[s * steps + u : s * steps + u + 1, side : side + head_dim]
                    merged = jnp.where(row + low == first + u, fresh_row, merged)
                tiles.append((pool, page, base, merged.astype(BF16)))
    for pool, page, base, merged in tiles:
        pool[page, pl.ds(base, tile), :] = merged

    stores = [
        pltpu.make_async_copy(kp, key_out, sems.at[0]),
        pltpu.make_async_copy(vp, value_out, sems.at[1]),
    ]
    for store in stores:
        store.start()
    attention = jnp.concatenate([a_scr[h * rows : (h + 1) * rows, :].astype(BF16) for h in range(heads)], 1)
    result = jnp.zeros((rows, wo.shape[1]), F32)
    size = wo.shape[0] // PARTS
    for part in range(PARTS):
        piece = slice(part * size, (part + 1) * size)
        load_wo[part].wait()
        result = result + jnp.dot(attention[:, piece], wo[piece, :], preferred_element_type=F32)
    partial[...] = result.astype(BF16)
    for store in stores:
        store.wait()


def finish_rows_kernel(groups, mig, lens, new_rows, *refs):
    *parts, mixed, near_out, far_out, scr = refs
    me = lax.axis_index("dec")
    slots = outgoing(mig, me, groups)
    width = parts[0].shape[1]
    terms = [part[...].astype(F32) for part in parts]
    level = 1
    while level < len(terms):
        terms = [terms[n] + terms[n ^ level] for n in range(len(terms))]
        level *= 2
    total = terms[0]
    slot_count, steps, _ = scr.shape
    for s in range(slot_count):
        live = (lens[me, s] > 0) & (s != slots[0]) & (s != slots[1])
        own = total[s * steps : (s + 1) * steps]
        scr[s, :, :width] = own
        scr[s, :, width:] = new_rows[s * steps : (s + 1) * steps, :].astype(F32)
        mixed[s] = jnp.where(live, own, 0.0).astype(BF16)
    for slot, out in zip(slots, (near_out, far_out)):
        out[...] = scr[jnp.maximum(slot, 0)].astype(BF16)


def place_kernel(groups, ways, mig, lens, table, *refs):
    near_pages, *far_pages = refs[: 1 + ways]
    near_rows, *far_rows = refs[1 + ways : 2 + 2 * ways]
    mixed_in, _, _, mixed, key_out, value_out, stage, lines, in_sems, line_sems, out_sems, own_sem = refs[
        2 + 2 * ways :
    ]
    me = lax.axis_index("dec")
    pages = table.shape[1]
    page_len, head_dim = stage.shape[2:]
    _, steps, width = mixed.shape
    *cases, far_gap = incoming(mig, lens, me, groups)
    row = lax.broadcasted_iota(jnp.int32, (page_len, head_dim), 0)

    def load(n, source):
        return pltpu.make_async_copy(source, stage.at[n], in_sems.at[n])

    def load_line(n, source):
        return pltpu.make_async_copy(source, lines.at[n], line_sems.at[n, 0])

    def store_line(n):
        return pltpu.make_async_copy(
            lines.at[n, :, pl.ds(0, width)], mixed.at[cases[n][0]], line_sems.at[n, 1]
        )

    def store(n, p, which):
        pool = (key_out, value_out)[which]
        page = table[0, p, cases[n][0]]
        return pltpu.make_async_copy(stage.at[n, which * pages + p], pool.at[page], out_sems.at[n, which, p])

    def each(do):
        for n in range(2):

            @pl.when(cases[n][0] >= 0)
            def _():
                do(n)

    def start(n):
        if n == 0 or ways == 1:
            load_line(n, (near_rows, far_rows[0])[n]).start()
            load(n, (near_pages, far_pages[0])[n]).start()
            return
        for way in range(ways):

            @pl.when((far_gap == 1) == (way == 0))
            def _():
                load_line(n, far_rows[way]).start()
                load(n, far_pages[way]).start()

    def patch(n):
        _, length = cases[n]
        load_line(n, near_rows).wait()
        store_line(n).start()
        fresh = lines[n, :, width:].astype(F32)
        load(n, near_pages).wait()
        for p in range(pages):
            at = row + p * page_len
            for which in range(2):
                page = stage[n, which * pages + p].astype(F32)
                page = jnp.where(at < length, page, 0.0)
                for t in range(steps):
                    page = jnp.where(
                        at == length + t, fresh[t : t + 1, which * head_dim : (which + 1) * head_dim], page
                    )
                stage[n, which * pages + p] = page.astype(BF16)
                store(n, p, which).start()

    def finish(n):
        store_line(n).wait()
        for p in range(pages):
            for which in range(2):
                store(n, p, which).wait()

    own = pltpu.make_async_copy(mixed_in, mixed, own_sem)
    own.start()
    each(start)
    own.wait()
    each(patch)
    each(finish)


def run(
    near_hops,
    far_hops,
    table,
    token_states,
    query_rows,
    key_weight,
    value_weight,
    out_weight,
    keys,
    values,
    cached_len,
    migrations,
):
    groups = lax.axis_size("dec")
    tp = lax.axis_size("tp")
    slot_count, steps, model = token_states.shape
    _, page_len, head_dim = keys.shape
    rows = slot_count * steps
    width = out_weight.shape[1]
    heads = query_rows.shape[2] // head_dim
    pages = table.shape[1]
    pool_shape = jax.ShapeDtypeStruct(keys.shape, BF16)
    moved_shape = jax.ShapeDtypeStruct((2 * pages, page_len, head_dim), BF16)
    limit = pltpu.CompilerParams(vmem_limit_bytes=63 * 2**20)

    near, far, token = pl.pallas_call(
        functools.partial(pack_kernel, groups),
        out_shape=(moved_shape, moved_shape, jax.ShapeDtypeStruct((1,), jnp.int32)),
        in_specs=[SMEM, SMEM, HBM, HBM],
        out_specs=(VMEM, VMEM, SMEM),
        scratch_shapes=[pltpu.SemaphoreType.DMA((2, 2, pages))],
        compiler_params=limit,
        name="pack",
    )(migrations, table, keys, values)
    pages_in = [lax.ppermute(near, "dec", near_hops)] + [lax.ppermute(far, "dec", hops) for hops in far_hops]

    key_mid, value_mid, partial, new_rows = pl.pallas_call(
        functools.partial(attend_kernel, groups),
        out_shape=(
            pool_shape,
            pool_shape,
            jax.ShapeDtypeStruct((rows, width), BF16),
            jax.ShapeDtypeStruct((rows, 2 * head_dim), BF16),
        ),
        in_specs=[SMEM, SMEM, SMEM, SMEM, VMEM, VMEM, HBM, HBM, HBM, HBM, HBM],
        out_specs=(HBM, HBM, VMEM, VMEM),
        scratch_shapes=[
            pltpu.VMEM(key_weight.shape, BF16),
            pltpu.VMEM(value_weight.shape, BF16),
            pltpu.VMEM(out_weight.shape, BF16),
            pltpu.VMEM(keys.shape, BF16),
            pltpu.VMEM(values.shape, BF16),
            pltpu.VMEM((heads * rows, head_dim), F32),
            pltpu.VMEM((heads * rows, head_dim), F32),
            pltpu.VMEM((rows, 2 * head_dim), F32),
            pltpu.SemaphoreType.DMA((5 * PARTS,)),
        ],
        compiler_params=pltpu.CompilerParams(vmem_limit_bytes=40 * 2**20),
        cost_estimate=pl.CostEstimate(flops=1_000_000, bytes_accessed=1_000_000, transcendentals=0),
        name="attend",
    )(
        token,
        migrations,
        cached_len,
        table,
        token_states,
        query_rows,
        key_weight,
        value_weight,
        out_weight,
        keys,
        values,
    )

    others = [lax.ppermute(partial, "tp", [(i, i ^ n) for i in range(tp)]) for n in range(1, tp)]
    row_shape = jax.ShapeDtypeStruct((steps, width + 2 * head_dim), BF16)
    mixed, near_row, far_row = pl.pallas_call(
        functools.partial(finish_rows_kernel, groups),
        out_shape=(jax.ShapeDtypeStruct((slot_count, steps, width), BF16), row_shape, row_shape),
        in_specs=[SMEM, SMEM, VMEM] + [VMEM] * tp,
        out_specs=(VMEM, VMEM, VMEM),
        scratch_shapes=[pltpu.VMEM((slot_count, steps, width + 2 * head_dim), F32)],
        compiler_params=pltpu.CompilerParams(vmem_limit_bytes=8 * 2**20),
        name="rows",
    )(migrations, cached_len, new_rows, partial, *others)
    rows_in = [lax.ppermute(near_row, "dec", near_hops)] + [lax.ppermute(far_row, "dec", hops) for hops in far_hops]
    return pages_in, rows_in, mixed, key_mid, value_mid


def moved(table, inputs):
    groups = lax.axis_size("dec")
    half = groups // 2
    if half != 2:
        return run(shifted(groups, half), (shifted(groups, 1), shifted(groups, 1 + half)), table, *inputs)
    source_group = inputs[-1][:, 0]
    branches = []
    for case in range(2**half):
        senders = [pair + half * (case >> pair & 1) for pair in range(half)]
        receivers = [(sender + half) % groups for sender in senders]
        near_hops = [(senders[pair], receivers[pair]) for pair in range(half)]
        far_hops = [(senders[pair], receivers[(pair + 1) % half]) for pair in range(half)]
        near_hops += [(b, a) for a, b in near_hops]
        far_hops += [(b, a) for a, b in far_hops]
        branches.append(functools.partial(run, near_hops, (far_hops,)))
    bits = jnp.where(source_group >= half, source_group - half + 1, 0)
    number = lax.reduce(bits, jnp.int32(0), lax.bitwise_or, (0,))
    return lax.switch(number, branches, table, *inputs)


def local(
    token_states,
    query_rows,
    key_weight,
    value_weight,
    out_weight,
    key_pool,
    value_pool,
    cached_len,
    page_table,
    migrations,
):
    groups = lax.axis_size("dec")
    pool_pages, _, page_len, head_dim = key_pool.shape
    slot_count, steps, _ = token_states.shape
    keys = key_pool.reshape(pool_pages, page_len, head_dim)
    values = value_pool.reshape(pool_pages, page_len, head_dim)
    table = jnp.swapaxes(page_table, 1, 2)
    pages = table.shape[1]
    inputs = (
        token_states,
        query_rows,
        key_weight,
        value_weight,
        out_weight,
        keys,
        values,
        cached_len,
        migrations,
    )
    pages_in, rows_in, mixed_mid, key_mid, value_mid = moved(table, inputs)
    ways = len(pages_in) - 1
    pool_shape = jax.ShapeDtypeStruct(keys.shape, BF16)
    mixed_shape = jax.ShapeDtypeStruct((slot_count, steps, out_weight.shape[1]), BF16)
    mixed, key_out, value_out = pl.pallas_call(
        functools.partial(place_kernel, groups, ways),
        out_shape=(mixed_shape, pool_shape, pool_shape),
        in_specs=[SMEM] * 3 + [ANY] * (2 + 2 * ways) + [VMEM] + [HBM] * 2,
        out_specs=(HBM, HBM, HBM),
        scratch_shapes=[
            pltpu.VMEM((2, 2 * pages, page_len, head_dim), BF16),
            pltpu.VMEM((2,) + rows_in[0].shape, BF16),
            pltpu.SemaphoreType.DMA((2,)),
            pltpu.SemaphoreType.DMA((2, 2)),
            pltpu.SemaphoreType.DMA((2, 2, pages)),
            pltpu.SemaphoreType.DMA,
        ],
        input_output_aliases={6 + 2 * ways: 1, 7 + 2 * ways: 2},
        compiler_params=pltpu.CompilerParams(vmem_limit_bytes=63 * 2**20),
        name="place",
    )(migrations, cached_len, table, *pages_in, *rows_in, mixed_mid, key_mid, value_mid)
    return mixed, key_out.reshape(key_pool.shape), value_out.reshape(value_pool.shape)


def solution(mesh):
    placed = (
        P(("rep", "dec"), None, None),
        P(("rep", "dec"), None, "tp"),
        P(None, "tp"),
        P(None, "tp"),
        P("tp", None),
        P(("rep", "dec"), "tp", None, None),
        P(("rep", "dec"), "tp", None, None),
        P("rep", None),
        P(("rep", "dec"), None, None),
        P("rep", None),
    )
    return jax.shard_map(
        local,
        mesh=mesh,
        in_specs=placed,
        out_specs=(
            P(("rep", "dec"), None, None),
            P(("rep", "dec"), "tp", None, None),
            P(("rep", "dec"), "tp", None, None),
        ),
        check_vma=False,
    )
```

profile of v0, /device:TPU:4, one launch (start us, length us, event | category | flops | bytes accessed | tf_op | source)
XLA Modules:
  0.0 36.1 jit_solution(2553436049078545795)
XLA Ops:
  0.6 1.3 %select_reduce_fusion = s32[]{:T(128)} fusion(s32[4,4]{1,0:T(4,128)} %mig.1), kind=kLoop, calls=%fused_computation | loop fusion | flops 15 | bytes 20 | tf_op jit(solution)/shard_map/reduce | solution.py:441
  2.6 30.3 %conditional.1 = (bf16[8,128,128]{2,1,0:T(8,128)(2,1)}, bf16[8,128,128]{2,1,0:T(8,128)(2,1)}, bf16[2,2816]{1,0:T(2,128)(2,1)}, bf16[2,2816]{1,0:T(2,128)(2,1)}, ...) conditional(s32[]{:T(128)} %clamp.3, (s32[4,4]{1,0:T(4,128)}, ...), branch_computations={%region_1.2_spmd, %region_2.3_spmd, %region_3.4_spmd, %region_4.5_... | conditional | flops 1000000 | bytes 4958492 | solution.py:442
  2.8 0.0 copy-start.3
  2.8 0.0 copy-start.7
  2.8 0.0 copy-start.11
  2.9 0.0 copy-start.15
  2.9 0.0 copy-start.19
  2.9 1.9 %pack.7 = (bf16[8,128,128]{2,1,0:T(8,128)(2,1)}, bf16[8,128,128]{2,1,0:T(8,128)(2,1)}, s32[1]{0:T(128)}) custom-call(s32[4,4]{1,0:T(4,128)} %get-tuple-element.140.mig, s32[1,4,8]{2,1,0:T(4,128)} %get-tuple-element.141.table, bf16[32,128,128]{2,1,0:T(8,128)(2,1)} %get-tuple-element.142.key_pool, bf16[32,128,128]{2,1,0:T(8,128)(2,1)} %get-tuple-element.143.value_pool), custom_call_target="tpu_custom_call" | custom-call | tf_op jit(solution)/shard_map/cond/branch_3_fun/pack/pallas_call | solution.py:361
  4.8 3.6 %collective-permute-start.21 = (bf16[8,128,128]{2,1,0:T(8,128)(2,1)}, bf16[8,128,128]{2,1,0:T(8,128)(2,1)}, u32[]{:S(2)}, u32[]{:S(2)}) collective-permute-start(bf16[8,128,128]{2,1,0:T(8,128)(2,1)} %get-tuple-element.144), channel_id=1, source_target_pairs={{8,0},{12,4},{0,8},{4,12},{9,1},{13,5},{1,9},{5,13},{10,2},{14,6},... | collective-permute-start | bytes 786440 | tf_op jit(solution)/shard_map/cond/branch_3_fun/ppermute | solution.py:370
  8.4 1.1 %collective-permute-start.22 = (bf16[8,128,128]{2,1,0:T(8,128)(2,1)}, bf16[8,128,128]{2,1,0:T(8,128)(2,1)}, u32[]{:S(2)}, u32[]{:S(2)}) collective-permute-start(bf16[8,128,128]{2,1,0:T(8,128)(2,1)} %get-tuple-element.145), channel_id=1, source_target_pairs={{8,4},{12,0},{4,8},{0,12},{9,5},{13,1},{5,9},{1,13},{10,6},{14,2},... | collective-permute-start | bytes 786440 | tf_op jit(solution)/shard_map/cond/branch_3_fun/ppermute | solution.py:370
  9.5 0.0 copy-done.3
  9.5 0.0 copy-done.7
  9.5 0.0 copy-done.11
  9.5 0.0 copy-done.15
  9.5 0.0 copy-done.19
  9.5 8.1 %attend.7 = (bf16[32,128,128]{2,1,0:T(8,128)(2,1)}, bf16[32,128,128]{2,1,0:T(8,128)(2,1)}, bf16[16,2560]{1,0:T(8,128)(2,1)S(1)}, bf16[16,256]{1,0:T(8,128)(2,1)S(1)}) custom-call(s32[1]{0:T(128)} %get-tuple-element.147.token, s32[4,4]{1,0:T(4,128)S(1)} %copy-done.11, s32[4,8]{1,0:T(4,128)S(1)} %copy-done.15, s32[1,4,8]{2,1,0:T(4,128)S(1)} %copy-done.19, ...), custom_call_target="tpu_custom_call" | custom-call | flops 1000000 | bytes 1000000 | tf_op jit(solution)/shard_map/cond/branch_3_fun/attend/pallas_call | solution.py:372
  17.7 0.7 %collective-permute-start.25 = (bf16[16,2560]{1,0:T(8,128)(2,1)S(1)}, bf16[16,2560]{1,0:T(8,128)(2,1)S(1)}, u32[]{:S(2)}, u32[]{:S(2)}) collective-permute-start(bf16[16,2560]{1,0:T(8,128)(2,1)S(1)} %get-tuple-element.154.refs_0_), channel_id=1, source_target_pairs={{0,3},{1,2},{2,1},{3,0},{4,7},{5,6},{6,5},{7,4},{8,11},{9,10},{10,... | collective-permute-start | bytes 245768 | tf_op jit(solution)/shard_map/cond/branch_3_fun/ppermute | solution.py:410
  18.4 0.9 %collective-permute-start.24 = (bf16[16,2560]{1,0:T(8,128)(2,1)S(1)}, bf16[16,2560]{1,0:T(8,128)(2,1)S(1)}, u32[]{:S(2)}, u32[]{:S(2)}) collective-permute-start(bf16[16,2560]{1,0:T(8,128)(2,1)S(1)} %get-tuple-element.154.refs_0_), channel_id=1, source_target_pairs={{0,2},{1,3},{2,0},{3,1},{4,6},{5,7},{6,4},{7,5},{8,10},{9,11},{10,... | collective-permute-start | bytes 245768 | tf_op jit(solution)/shard_map/cond/branch_3_fun/ppermute | solution.py:410
  19.3 0.3 collective-permute-start.23
  19.6 2.8 %collective-permute-done.25.refs_3_ = bf16[16,2560]{1,0:T(8,128)(2,1)S(1)} collective-permute-done((bf16[16,2560]{1,0:T(8,128)(2,1)S(1)}, bf16[16,2560]{1,0:T(8,128)(2,1)S(1)}, u32[]{:S(2)}, u32[]{:S(2)}) %collective-permute-start.25) | collective-permute-done | bytes 81952 | tf_op jit(solution)/shard_map/cond/branch_3_fun/ppermute | solution.py:410
  22.4 1.8 %collective-permute-done.24.refs_2_ = bf16[16,2560]{1,0:T(8,128)(2,1)S(1)} collective-permute-done((bf16[16,2560]{1,0:T(8,128)(2,1)S(1)}, bf16[16,2560]{1,0:T(8,128)(2,1)S(1)}, u32[]{:S(2)}, u32[]{:S(2)}) %collective-permute-start.24) | collective-permute-done | bytes 81952 | tf_op jit(solution)/shard_map/cond/branch_3_fun/ppermute | solution.py:410
  24.2 0.0 collective-permute-done.23.refs_1_
  24.2 0.7 %rows.7 = (bf16[8,2,2560]{2,1,0:T(2,128)(2,1)S(1)}, bf16[2,2816]{1,0:T(2,128)(2,1)S(1)}, bf16[2,2816]{1,0:T(2,128)(2,1)S(1)}) custom-call(s32[4,4]{1,0:T(4,128)S(1)} %copy-done.11, s32[4,8]{1,0:T(4,128)S(1)} %copy-done.15, bf16[16,256]{1,0:T(8,128)(2,1)S(1)} %get-tuple-element.153.new_rows, bf16[16,2560]{1,0:T(8,128)(2,1)S(1)} %get-tuple-element.154.refs_0_, ...), custom_call_target="tpu_custom_call" | custom-call | tf_op jit(solution)/shard_map/cond/branch_3_fun/rows/pallas_call | solution.py:412
  25.0 2.0 %collective-permute-start.26 = (bf16[2,2816]{1,0:T(2,128)(2,1)S(1)}, bf16[2,2816]{1,0:T(2,128)(2,1)}, u32[]{:S(2)}, u32[]{:S(2)}) collective-permute-start(bf16[2,2816]{1,0:T(2,128)(2,1)S(1)} %get-tuple-element.155), channel_id=1, source_target_pairs={{8,0},{12,4},{0,8},{4,12},{9,1},{13,5},{1,9},{5,13},{10,2},{14,6},... | collective-permute-start | bytes 33800 | tf_op jit(solution)/shard_map/cond/branch_3_fun/ppermute | solution.py:421
  27.0 0.9 %collective-permute-start.27 = (bf16[2,2816]{1,0:T(2,128)(2,1)S(1)}, bf16[2,2816]{1,0:T(2,128)(2,1)}, u32[]{:S(2)}, u32[]{:S(2)}) collective-permute-start(bf16[2,2816]{1,0:T(2,128)(2,1)S(1)} %get-tuple-element.156), channel_id=1, source_target_pairs={{8,4},{12,0},{4,8},{0,12},{9,5},{13,1},{5,9},{1,13},{10,6},{14,2},... | collective-permute-start | bytes 33800 | tf_op jit(solution)/shard_map/cond/branch_3_fun/ppermute | solution.py:421
  27.9 4.8 %collective-permute-done.26 = bf16[2,2816]{1,0:T(2,128)(2,1)} collective-permute-done((bf16[2,2816]{1,0:T(2,128)(2,1)S(1)}, bf16[2,2816]{1,0:T(2,128)(2,1)}, u32[]{:S(2)}, u32[]{:S(2)}) %collective-permute-start.26) | collective-permute-done | bytes 11296 | tf_op jit(solution)/shard_map/cond/branch_3_fun/ppermute | solution.py:421
  32.7 0.0 collective-permute-done.27
  32.7 0.0 collective-permute-done.21
  32.7 0.0 collective-permute-done.22
  33.0 2.9 %place.1 = (bf16[8,2,2560]{2,1,0:T(2,128)(2,1)}, bf16[32,128,128]{2,1,0:T(8,128)(2,1)}, bf16[32,128,128]{2,1,0:T(8,128)(2,1)}) custom-call(s32[4,4]{1,0:T(4,128)} %mig.1, s32[4,8]{1,0:T(4,128)} %lens.1, s32[1,4,8]{2,1,0:T(4,128)} %bitcast.21, bf16[8,128,128]{2,1,0:T(8,128)(2,1)} %get-tuple-element.173.refs_0_, ...), custom_call_target="tpu_custom_call", output_to_operand_aliasing={{1}: (8, {}), {2}: (9, {})} | custom-call | tf_op jit(solution)/shard_map/place/pallas_call | solution.py:479
Async XLA Ops:
  2.8 6.7 %copy-start.3 = (bf16[8,2,5120]{2,1,0:T(2,128)(2,1)S(1)}, bf16[8,2,5120]{2,1,0:T(2,128)(2,1)}, u32[]{:S(2)}) copy-start(bf16[8,2,5120]{2,1,0:T(2,128)(2,1)} %get-tuple-element.148.states) | copy-start | bytes 491524 | tf_op jit(solution)/shard_map/cond
  2.8 6.7 %copy-start.7 = (bf16[8,2,1024]{2,1,0:T(2,128)(2,1)S(1)}, bf16[8,2,1024]{2,1,0:T(2,128)(2,1)}, u32[]{:S(2)}) copy-start(bf16[8,2,1024]{2,1,0:T(2,128)(2,1)} %get-tuple-element.149.query) | copy-start | bytes 98308 | tf_op jit(solution)/shard_map/cond
  2.8 6.7 %copy-start.11 = (s32[4,4]{1,0:T(4,128)S(1)}, s32[4,4]{1,0:T(4,128)}, u32[]{:S(2)}) copy-start(s32[4,4]{1,0:T(4,128)} %get-tuple-element.140.mig) | copy-start | bytes 196 | tf_op jit(solution)/shard_map/cond
  2.9 6.7 %copy-start.15 = (s32[4,8]{1,0:T(4,128)S(1)}, s32[4,8]{1,0:T(4,128)}, u32[]{:S(2)}) copy-start(s32[4,8]{1,0:T(4,128)} %get-tuple-element.146.lens) | copy-start | bytes 388 | tf_op jit(solution)/shard_map/cond
  2.9 6.6 %copy-start.19 = (s32[1,4,8]{2,1,0:T(4,128)S(1)}, s32[1,4,8]{2,1,0:T(4,128)}, u32[]{:S(2)}) copy-start(s32[1,4,8]{2,1,0:T(4,128)} %get-tuple-element.141.table) | copy-start | bytes 388 | tf_op jit(solution)/shard_map/cond
  4.8 27.9 %collective-permute-start.21 = (bf16[8,128,128]{2,1,0:T(8,128)(2,1)}, bf16[8,128,128]{2,1,0:T(8,128)(2,1)}, u32[]{:S(2)}, u32[]{:S(2)}) collective-permute-start(bf16[8,128,128]{2,1,0:T(8,128)(2,1)} %get-tuple-element.144), channel_id=1, source_target_pairs={{8,0},{12,4},{0,8},{4,12},{9,1},{13,5},{1,9},{5,13},{10,2},{14,6},... | collective-permute-start | bytes 786440 | tf_op jit(solution)/shard_map/cond/branch_3_fun/ppermute | solution.py:370
  8.4 24.3 %collective-permute-start.22 = (bf16[8,128,128]{2,1,0:T(8,128)(2,1)}, bf16[8,128,128]{2,1,0:T(8,128)(2,1)}, u32[]{:S(2)}, u32[]{:S(2)}) collective-permute-start(bf16[8,128,128]{2,1,0:T(8,128)(2,1)} %get-tuple-element.145), channel_id=1, source_target_pairs={{8,4},{12,0},{4,8},{0,12},{9,5},{13,1},{5,9},{1,13},{10,6},{14,2},... | collective-permute-start | bytes 786440 | tf_op jit(solution)/shard_map/cond/branch_3_fun/ppermute | solution.py:370
  17.7 4.8 %collective-permute-start.25 = (bf16[16,2560]{1,0:T(8,128)(2,1)S(1)}, bf16[16,2560]{1,0:T(8,128)(2,1)S(1)}, u32[]{:S(2)}, u32[]{:S(2)}) collective-permute-start(bf16[16,2560]{1,0:T(8,128)(2,1)S(1)} %get-tuple-element.154.refs_0_), channel_id=1, source_target_pairs={{0,3},{1,2},{2,1},{3,0},{4,7},{5,6},{6,5},{7,4},{8,11},{9,10},{10,... | collective-permute-start | bytes 245768 | tf_op jit(solution)/shard_map/cond/branch_3_fun/ppermute | solution.py:410
  18.4 5.8 %collective-permute-start.24 = (bf16[16,2560]{1,0:T(8,128)(2,1)S(1)}, bf16[16,2560]{1,0:T(8,128)(2,1)S(1)}, u32[]{:S(2)}, u32[]{:S(2)}) collective-permute-start(bf16[16,2560]{1,0:T(8,128)(2,1)S(1)} %get-tuple-element.154.refs_0_), channel_id=1, source_target_pairs={{0,2},{1,3},{2,0},{3,1},{4,6},{5,7},{6,4},{7,5},{8,10},{9,11},{10,... | collective-permute-start | bytes 245768 | tf_op jit(solution)/shard_map/cond/branch_3_fun/ppermute | solution.py:410
  19.3 4.9 %collective-permute-start.23 = (bf16[16,2560]{1,0:T(8,128)(2,1)S(1)}, bf16[16,2560]{1,0:T(8,128)(2,1)S(1)}, u32[]{:S(2)}, u32[]{:S(2)}) collective-permute-start(bf16[16,2560]{1,0:T(8,128)(2,1)S(1)} %get-tuple-element.154.refs_0_), channel_id=1, source_target_pairs={{0,1},{1,0},{2,3},{3,2},{4,5},{5,4},{6,7},{7,6},{8,9},{9,8},{10,11... | collective-permute-start | bytes 245768 | tf_op jit(solution)/shard_map/cond/branch_3_fun/ppermute | solution.py:410
  25.0 7.7 %collective-permute-start.26 = (bf16[2,2816]{1,0:T(2,128)(2,1)S(1)}, bf16[2,2816]{1,0:T(2,128)(2,1)}, u32[]{:S(2)}, u32[]{:S(2)}) collective-permute-start(bf16[2,2816]{1,0:T(2,128)(2,1)S(1)} %get-tuple-element.155), channel_id=1, source_target_pairs={{8,0},{12,4},{0,8},{4,12},{9,1},{13,5},{1,9},{5,13},{10,2},{14,6},... | collective-permute-start | bytes 33800 | tf_op jit(solution)/shard_map/cond/branch_3_fun/ppermute | solution.py:421
  27.0 5.7 %collective-permute-start.27 = (bf16[2,2816]{1,0:T(2,128)(2,1)S(1)}, bf16[2,2816]{1,0:T(2,128)(2,1)}, u32[]{:S(2)}, u32[]{:S(2)}) collective-permute-start(bf16[2,2816]{1,0:T(2,128)(2,1)S(1)} %get-tuple-element.156), channel_id=1, source_target_pairs={{8,4},{12,0},{4,8},{0,12},{9,5},{13,1},{5,9},{1,13},{10,6},{14,2},... | collective-permute-start | bytes 33800 | tf_op jit(solution)/shard_map/cond/branch_3_fun/ppermute | solution.py:421
where the time goes:
time: 36.3 us; the launch traced here: 36.1 us
  Pallas kernels  13.7 us (38%)
  starting transfers between devices  9.54 us (26%)
  waiting for transfers between devices  9.47 us (26%)
  between operations  1.47 us (4%)
  other arithmetic  1.32 us (4%)
  loops' own time  0.51 us (1%)
    pallas_call x1, Pallas kernels, run(): pl.pallas_call(functools.partial(attend_kernel, groups), out_shape=(pool_...  8.13 us
    ppermute x1, waiting for transfers between devices, run(): lax.ppermute(near_row, 'dec', near_hops)  4.82 us
    ppermute x3, waiting for transfers between devices, run(): lax.ppermute(partial, 'tp', [(i, i ^ n) for i in range(tp)])  4.64 us
    ppermute x1, starting transfers between devices, run(): lax.ppermute(near, 'dec', near_hops)  3.59 us
    pallas_call x1, Pallas kernels, local(): pl.pallas_call(functools.partial(place_kernel, groups, ways), out_shape=(...  2.91 us
    ppermute x1, starting transfers between devices, run(): lax.ppermute(near_row, 'dec', near_hops)  2.01 us
    pallas_call x1, Pallas kernels, run(): pl.pallas_call(functools.partial(pack_kernel, groups), out_shape=(moved_s...  1.93 us
    ppermute x3, starting transfers between devices, run(): lax.ppermute(partial, 'tp', [(i, i ^ n) for i in range(tp)])  1.93 us
  transfers between devices with their start and end apart: 7, of which 3 were waited for; matrix products, arithmetic and copies ran while one was open for 0% of the time, Pallas kernels for 25%

commit v1 on v0

--- a/solution.py
+++ b/solution.py
@@ -80,26 +80,28 @@
     mig,
     lens,
     table,
-    states,
-    query,
+    states_hbm,
+    query_hbm,
     key_weight,
     value_weight,
     out_weight,
-    key_pool,
-    value_pool,
+    kp,
+    vp,
     key_out,
     value_out,
     partial,
     new_rows,
+    states,
+    query,
     wk,
     wv,
     wo,
-    kp,
-    vp,
     q_scr,
     a_scr,
-    n_scr,
-    sems,
+    tiles,
+    load_sems,
+    store_sems,
+    tile_sems,
 ):
     del token
     me = lax.axis_index("dec")
@@ -109,6 +111,7 @@
     page_len, head_dim = kp.shape[1:]
     heads = query.shape[2] // head_dim
     span = pages * page_len
+    pools = ((kp, key_out, 0), (vp, value_out, head_dim))
     number = 0
 
     def split(source, target, parts):
@@ -117,47 +120,46 @@
         copies = []
         for part in range(parts):
             piece = pl.ds(part * size, size)
-            copies.append(pltpu.make_async_copy(source.at[piece], target.at[piece], sems.at[number]))
+            copies.append(pltpu.make_async_copy(source.at[piece], target.at[piece], load_sems.at[number]))
             number += 1
         return copies
 
-    load_keys = split(key_pool, kp, PARTS)
+    (load_query,) = split(query_hbm, query, 1)
+    (load_states,) = split(states_hbm, states, 1)
     load_wk = split(key_weight, wk, PARTS)
     load_wv = split(value_weight, wv, PARTS)
-    load_values = split(value_pool, vp, PARTS)
-    load_wo = split(out_weight, wo, PARTS)
-    for load in load_keys + load_wk + load_wv + load_values + load_wo:
-        load.start()
+    loads = split(out_weight, wo, PARTS)
+    stores = [pltpu.make_async_copy(pool, out, store_sems.at[n]) for n, (pool, out, _) in enumerate(pools)]
+    for copy in [load_query, load_states] + load_wk + load_wv + loads + stores:
+        copy.start()
     near, far = outgoing(mig, me, groups)
     lengths = [lens[me, s] for s in range(slot_count)]
-
+    numbers = [[table[0, p, s] for p in range(pages)] for s in range(slot_count)]
+
+    load_query.wait()
     for s in range(slot_count):
         qf = query[s].astype(F32)
         for h in range(heads):
             q_scr[pl.ds(h * rows + s * steps, steps), :] = qf[:, h * head_dim : (h + 1) * head_dim]
-    x = jnp.concatenate([states[s].astype(F32) for s in range(slot_count)], 0).astype(BF16)
-    queries = [
-        jnp.concatenate(
-            [q_scr[pl.ds(s * steps + t, heads, stride=rows), :] for t in range(steps)], 0
-        ).astype(BF16)
-        for s in range(slot_count)
-    ]
-
+
+    count = steps * heads
+    nt = (((1,), (1,)), ((), ()))
+    queries = jnp.concatenate(
+        [q_scr[pl.ds(r, heads, stride=rows), :] for r in range(rows)], 0
+    ).astype(BF16)
+    position = lax.broadcasted_iota(jnp.int32, (count, span), 1)
     scaling = head_dim**-0.5
-    count = steps * heads
-    fresh_col = lax.broadcasted_iota(jnp.int32, (count, rows), 1)
-    fresh_step = lax.broadcasted_iota(jnp.int32, (count, rows), 0) // heads
-    position = lax.broadcasted_iota(jnp.int32, (count, span), 1)
-    nt = (((1,), (1,)), ((), ()))
-    numbers = [[table[0, p, s] for p in range(pages)] for s in range(slot_count)]
-    for load in load_keys:
-        load.wait()
     scores = []
     for s in range(slot_count):
         keys = jnp.concatenate([kp[n] for n in numbers[s]], 0)
-        cached = lax.dot_general(queries[s], keys, nt, preferred_element_type=F32) * scaling
-        scores.append(jnp.where(position < lengths[s], cached, -jnp.inf))
-
+        cached = lax.dot_general(
+            queries[s * count : (s + 1) * count], keys, nt, preferred_element_type=F32
+        )
+        scores.append(jnp.where(position < lengths[s], cached * scaling, -jnp.inf))
+    cached = jnp.concatenate(scores, 0)
+
+    load_states.wait()
+    x = jnp.concatenate([states[s].astype(F32) for s in range(slot_count)], 0).astype(BF16)
     fresh_k = jnp.zeros((rows, head_dim), F32)
     fresh_v = jnp.zeros((rows, head_dim), F32)
     size = wk.shape[0] // PARTS
@@ -167,67 +169,78 @@
         fresh_k = fresh_k + jnp.dot(x[:, piece], wk[piece, :], preferred_element_type=F32)
         load_wv[part].wait()
         fresh_v = fresh_v + jnp.dot(x[:, piece], wv[piece, :], preferred_element_type=F32)
-    fresh_rows = jnp.concatenate([fresh_k, fresh_v], 1).astype(BF16)
-    new_rows[...] = fresh_rows
-    n_scr[...] = fresh_rows.astype(F32)
-    new_k = fresh_rows[:, :head_dim]
-    new_v = fresh_rows[:, head_dim:]
-
-    for load in load_values:
-        load.wait()
+    fresh_k = fresh_k.astype(BF16)
+    fresh_v = fresh_v.astype(BF16)
+    new_rows[:, :head_dim] = fresh_k
+    new_rows[:, head_dim:] = fresh_v
+
+    fresh = lax.dot_general(queries, fresh_k, nt, preferred_element_type=F32) * scaling
+    fresh_row = lax.broadcasted_iota(jnp.int32, fresh.shape, 0)
+    fresh_col = lax.broadcasted_iota(jnp.int32, fresh.shape, 1)
+    first = fresh_row // count * steps
+    allowed = (fresh_col >= first) & (fresh_col <= fresh_row // heads)
+    fresh = jnp.where(allowed, fresh, -jnp.inf)
+    peak = jnp.maximum(jnp.max(cached, 1, keepdims=True), jnp.max(fresh, 1, keepdims=True))
+    cached = jnp.exp(cached - peak)
+    fresh = jnp.exp(fresh - peak)
+    share = 1.0 / (jnp.sum(cached, 1, keepdims=True) + jnp.sum(fresh, 1, keepdims=True))
+    cached_w = (cached * share).astype(BF16)
+    fresh_w = (fresh * share).astype(BF16)
+    fresh_out = jnp.dot(fresh_w, fresh_v, preferred_element_type=F32)
     for s in range(slot_count):
         values = jnp.concatenate([vp[n] for n in numbers[s]], 0)
-        cached = scores[s]
-        fresh = lax.dot_general(queries[s], new_k, nt, preferred_element_type=F32) * scaling
-        ok = (fresh_col >= s * steps) & (fresh_col <= s * steps + fresh_step)
-        fresh = jnp.where(ok, fresh, -jnp.inf)
-        peak = jnp.maximum(jnp.max(cached, 1, keepdims=True), jnp.max(fresh, 1, keepdims=True))
-        cached = jnp.exp(cached - peak)
-        fresh = jnp.exp(fresh - peak)
-        total = jnp.sum(cached, 1, keepdims=True) + jnp.sum(fresh, 1, keepdims=True)
-        cached_w = (cached / total).astype(BF16)
-        fresh_w = (fresh / total).astype(BF16)
-        out = jnp.dot(cached_w, values, preferred_element_type=F32)
-        out = out + jnp.dot(fresh_w, new_v, preferred_element_type=F32)
+        piece = slice(s * count, (s + 1) * count)
+        out = jnp.dot(cached_w[piece], values, preferred_element_type=F32) + fresh_out[piece]
         for t in range(steps):
             a_scr[pl.ds(s * steps + t, heads, stride=rows), :] = out[t * heads : (t + 1) * heads]
 
-    tile = 16
+    tile = tiles.shape[3]
     row = lax.broadcasted_iota(jnp.int32, (tile, head_dim), 0)
-    tiles = []
+    fresh_f = (fresh_k.astype(F32), fresh_v.astype(F32))
+    places = []
     for s in range(slot_count):
         live = (lengths[s] > 0) & (s != near) & (s != far)
-        first = jnp.where(live, lengths[s], -steps)
         for t in range(steps):
             at = lengths[s] + t
             page = table[0, at // page_len, s]
             low = at // tile * tile
             base = pl.multiple_of(lax.rem(low, page_len), tile)
-            for pool, side in ((kp, 0), (vp, head_dim)):
+            places.append((s, t, page, base, live & ((t == 0) | (lax.rem(at, tile) == 0))))
+            for n, (pool, _, _) in enumerate(pools):
                 merged = pool[page, pl.ds(base, tile), :].astype(F32)
                 for u in range(steps):
-                    fresh_row = n_scr[s * steps + u : s * steps + u + 1, side : side + head_dim]
-                    merged = jnp.where(row + low == first + u, fresh_row, merged)
-                tiles.append((pool, page, base, merged.astype(BF16)))
-    for pool, page, base, merged in tiles:
-        pool[page, pl.ds(base, tile), :] = merged
-
-    stores = [
-        pltpu.make_async_copy(kp, key_out, sems.at[0]),
-        pltpu.make_async_copy(vp, value_out, sems.at[1]),
-    ]
+                    line = fresh_f[n][s * steps + u : s * steps + u + 1]
+                    merged = jnp.where(row + low == lengths[s] + u, line, merged)
+                tiles[n, s, t] = merged.astype(BF16)
     for store in stores:
-        store.start()
+        store.wait()
+
+    def put(n, s, t, page, base):
+        return pltpu.make_async_copy(
+            tiles.at[n, s, t], pools[n][1].at[page, pl.ds(base, tile), :], tile_sems.at[n, s, t]
+        )
+
+    for s, t, page, base, wanted in places:
+
+        @pl.when(wanted)
+        def _():
+            for n in range(2):
+                put(n, s, t, page, base).start()
+
     attention = jnp.concatenate([a_scr[h * rows : (h + 1) * rows, :].astype(BF16) for h in range(heads)], 1)
     result = jnp.zeros((rows, wo.shape[1]), F32)
     size = wo.shape[0] // PARTS
     for part in range(PARTS):
         piece = slice(part * size, (part + 1) * size)
-        load_wo[part].wait()
+        loads[part].wait()
         result = result + jnp.dot(attention[:, piece], wo[piece, :], preferred_element_type=F32)
     partial[...] = result.astype(BF16)
-    for store in stores:
-        store.wait()
+    for s, t, page, base, wanted in places:
+
+        @pl.when(wanted)
+        def _():
+            for n in range(2):
+                put(n, s, t, page, base).wait()
 
 
 def finish_rows_kernel(groups, mig, lens, new_rows, *refs):
@@ -364,7 +377,8 @@
         in_specs=[SMEM, SMEM, HBM, HBM],
         out_specs=(VMEM, VMEM, SMEM),
         scratch_shapes=[pltpu.SemaphoreType.DMA((2, 2, pages))],
-        compiler_params=limit,
+        compiler_params=pltpu.CompilerParams(vmem_limit_bytes=40 * 2**20),
+        cost_estimate=pl.CostEstimate(flops=0, bytes_accessed=1_000_000, transcendentals=0),
         name="pack",
     )(migrations, table, keys, values)
     pages_in = [lax.ppermute(near, "dec", near_hops)] + [lax.ppermute(far, "dec", hops) for hops in far_hops]
@@ -377,18 +391,20 @@
             jax.ShapeDtypeStruct((rows, width), BF16),
             jax.ShapeDtypeStruct((rows, 2 * head_dim), BF16),
         ),
-        in_specs=[SMEM, SMEM, SMEM, SMEM, VMEM, VMEM, HBM, HBM, HBM, HBM, HBM],
+        in_specs=[SMEM] * 4 + [ANY] * 5 + [VMEM] * 2,
         out_specs=(HBM, HBM, VMEM, VMEM),
         scratch_shapes=[
+            pltpu.VMEM(token_states.shape, BF16),
+            pltpu.VMEM(query_rows.shape, BF16),
             pltpu.VMEM(key_weight.shape, BF16),
             pltpu.VMEM(value_weight.shape, BF16),
             pltpu.VMEM(out_weight.shape, BF16),
-            pltpu.VMEM(keys.shape, BF16),
-            pltpu.VMEM(values.shape, BF16),
             pltpu.VMEM((heads * rows, head_dim), F32),
             pltpu.VMEM((heads * rows, head_dim), F32),
-            pltpu.VMEM((rows, 2 * head_dim), F32),
-            pltpu.SemaphoreType.DMA((5 * PARTS,)),
+            pltpu.VMEM((2, slot_count, steps, 16, head_dim), BF16),
+            pltpu.SemaphoreType.DMA((2 + 3 * PARTS,)),
+            pltpu.SemaphoreType.DMA((2,)),
+            pltpu.SemaphoreType.DMA((2, slot_count, steps)),
         ],
         compiler_params=pltpu.CompilerParams(vmem_limit_bytes=40 * 2**20),
         cost_estimate=pl.CostEstimate(flops=1_000_000, bytes_accessed=1_000_000, transcendentals=0),

time: 36.3 us -> 35.8 us (0.986)
  Pallas kernels: 13.7 us -> 11.8 us
  waiting for transfers between devices: 9.47 us -> 10.9 us
    pallas_call x1, Pallas kernels: 8.13 us -> 6.48 us  [run(): pl.pallas_call(functools.partial(attend_kernel, groups), out_shape=(pool_...]
    ppermute x1, waiting for transfers between devices: 4.82 us -> 6.26 us  [run(): lax.ppermute(near_row, 'dec', near_hops)]
  transfers between devices with their start and end apart: 7 -> 7, of which waited for: 3 -> 3; matrix products, arithmetic and copies ran while one was open for 0% -> 0% of each run, Pallas kernels for 25% -> 20%
where the time goes in v1:
time: 35.8 us; the launch traced here: 35.5 us
  Pallas kernels  11.8 us (33%)
  waiting for transfers between devices  10.9 us (30%)
  starting transfers between devices  9.53 us (27%)
  between operations  1.47 us (4%)
  other arithmetic  1.32 us (4%)
  loops' own time  0.51 us (1%)
    pallas_call x1, Pallas kernels, run(): pl.pallas_call(functools.partial(attend_kernel, groups), out_shape=(pool_...  6.48 us
    ppermute x1, waiting for transfers between devices, run(): lax.ppermute(near_row, 'dec', near_hops)  6.26 us
    ppermute x3, waiting for transfers between devices, run(): lax.ppermute(partial, 'tp', [(i, i ^ n) for i in range(tp)])  4.64 us
    ppermute x1, starting transfers between devices, run(): lax.ppermute(near, 'dec', near_hops)  3.59 us
    pallas_call x1, Pallas kernels, local(): pl.pallas_call(functools.partial(place_kernel, groups, ways), out_shape=(...  2.91 us
    ppermute x1, starting transfers between devices, run(): lax.ppermute(near_row, 'dec', near_hops)  2.01 us
    ppermute x3, starting transfers between devices, run(): lax.ppermute(partial, 'tp', [(i, i ^ n) for i in range(tp)])  1.93 us
    pallas_call x1, Pallas kernels, run(): pl.pallas_call(functools.partial(pack_kernel, groups), out_shape=(moved_s...  1.62 us
  transfers between devices with their start and end apart: 7, of which 3 were waited for; matrix products, arithmetic and copies ran while one was open for 0% of the time, Pallas kernels for 20%

profile of v1, /device:TPU:4, one launch (start us, length us, event | category | flops | bytes accessed | tf_op | source)
XLA Modules:
  0.0 35.5 jit_solution(17813498099795263973)
XLA Ops:
  0.6 1.3 %select_reduce_fusion = s32[]{:T(128)} fusion(s32[4,4]{1,0:T(4,128)} %mig.1), kind=kLoop, calls=%fused_computation | loop fusion | flops 15 | bytes 20 | tf_op jit(solution)/shard_map/reduce | solution.py:457
  2.6 29.8 %conditional.1 = (bf16[8,128,128]{2,1,0:T(8,128)(2,1)}, bf16[8,128,128]{2,1,0:T(8,128)(2,1)}, bf16[2,2816]{1,0:T(2,128)(2,1)}, bf16[2,2816]{1,0:T(2,128)(2,1)}, ...) conditional(s32[]{:T(128)} %clamp.3, (s32[4,4]{1,0:T(4,128)}, ...), branch_computations={%region_1.2_spmd, %region_2.3_spmd, %region_3.4_spmd, %region_4.5_... | conditional | flops 1000000 | bytes 13560668 | solution.py:458
  2.8 0.0 copy-start.3
  2.8 0.0 copy-start.7
  2.8 0.0 copy-start.11
  2.9 0.0 copy-start.15
  2.9 0.0 copy-start.19
  2.9 1.6 %pack.7 = (bf16[8,128,128]{2,1,0:T(8,128)(2,1)S(1)}, bf16[8,128,128]{2,1,0:T(8,128)(2,1)S(1)}, s32[1]{0:T(128)}) custom-call(s32[4,4]{1,0:T(4,128)} %get-tuple-element.140.mig, s32[1,4,8]{2,1,0:T(4,128)} %get-tuple-element.141.table, bf16[32,128,128]{2,1,0:T(8,128)(2,1)} %get-tuple-element.142.key_pool.kp, bf16[32,128,128]{2,1,0:T(8,128)(2,1)} %get-tuple-element.143.value_pool.vp), custom_call_target="tpu_custom_call" | custom-call | bytes 1000000 | tf_op jit(solution)/shard_map/cond/branch_3_fun/pack/pallas_call | solution.py:374
  4.5 3.6 %collective-permute-start.21 = (bf16[8,128,128]{2,1,0:T(8,128)(2,1)S(1)}, bf16[8,128,128]{2,1,0:T(8,128)(2,1)}, u32[]{:S(2)}, u32[]{:S(2)}) collective-permute-start(bf16[8,128,128]{2,1,0:T(8,128)(2,1)S(1)} %get-tuple-element.144), channel_id=1, source_target_pairs={{8,0},{12,4},{0,8},{4,12},{9,1},{13,5},{1,9},{5,13},{10,2},{14,6},... | collective-permute-start | bytes 786440 | tf_op jit(solution)/shard_map/cond/branch_3_fun/ppermute | solution.py:384
  8.1 1.1 %collective-permute-start.22 = (bf16[8,128,128]{2,1,0:T(8,128)(2,1)S(1)}, bf16[8,128,128]{2,1,0:T(8,128)(2,1)}, u32[]{:S(2)}, u32[]{:S(2)}) collective-permute-start(bf16[8,128,128]{2,1,0:T(8,128)(2,1)S(1)} %get-tuple-element.145), channel_id=1, source_target_pairs={{8,4},{12,0},{4,8},{0,12},{9,5},{13,1},{5,9},{1,13},{10,6},{14,2},... | collective-permute-start | bytes 786440 | tf_op jit(solution)/shard_map/cond/branch_3_fun/ppermute | solution.py:384
  9.2 0.0 copy-done.3
  9.2 0.0 copy-done.7
  9.2 0.0 copy-done.11
  9.2 0.0 copy-done.15
  9.2 0.0 copy-done.19
  9.2 6.5 %attend.7 = (bf16[32,128,128]{2,1,0:T(8,128)(2,1)}, bf16[32,128,128]{2,1,0:T(8,128)(2,1)}, bf16[16,2560]{1,0:T(8,128)(2,1)S(1)}, bf16[16,256]{1,0:T(8,128)(2,1)S(1)}) custom-call(s32[1]{0:T(128)} %get-tuple-element.147.token, s32[4,4]{1,0:T(4,128)S(1)} %copy-done.11, s32[4,8]{1,0:T(4,128)S(1)} %copy-done.15, s32[1,4,8]{2,1,0:T(4,128)S(1)} %copy-done.19, ...), custom_call_target="tpu_custom_call" | custom-call | flops 1000000 | bytes 1000000 | tf_op jit(solution)/shard_map/cond/branch_3_fun/attend/pallas_call | solution.py:386
  15.7 0.7 %collective-permute-start.25 = (bf16[16,2560]{1,0:T(8,128)(2,1)S(1)}, bf16[16,2560]{1,0:T(8,128)(2,1)S(1)}, u32[]{:S(2)}, u32[]{:S(2)}) collective-permute-start(bf16[16,2560]{1,0:T(8,128)(2,1)S(1)} %get-tuple-element.154.refs_0_), channel_id=1, source_target_pairs={{0,3},{1,2},{2,1},{3,0},{4,7},{5,6},{6,5},{7,4},{8,11},{9,10},{10,... | collective-permute-start | bytes 245768 | tf_op jit(solution)/shard_map/cond/branch_3_fun/ppermute | solution.py:426
  16.4 0.9 %collective-permute-start.24 = (bf16[16,2560]{1,0:T(8,128)(2,1)S(1)}, bf16[16,2560]{1,0:T(8,128)(2,1)S(1)}, u32[]{:S(2)}, u32[]{:S(2)}) collective-permute-start(bf16[16,2560]{1,0:T(8,128)(2,1)S(1)} %get-tuple-element.154.refs_0_), channel_id=1, source_target_pairs={{0,2},{1,3},{2,0},{3,1},{4,6},{5,7},{6,4},{7,5},{8,10},{9,11},{10,... | collective-permute-start | bytes 245768 | tf_op jit(solution)/shard_map/cond/branch_3_fun/ppermute | solution.py:426
  17.3 0.3 collective-permute-start.23
  17.6 2.8 %collective-permute-done.25.refs_3_ = bf16[16,2560]{1,0:T(8,128)(2,1)S(1)} collective-permute-done((bf16[16,2560]{1,0:T(8,128)(2,1)S(1)}, bf16[16,2560]{1,0:T(8,128)(2,1)S(1)}, u32[]{:S(2)}, u32[]{:S(2)}) %collective-permute-start.25) | collective-permute-done | bytes 81952 | tf_op jit(solution)/shard_map/cond/branch_3_fun/ppermute | solution.py:426
  20.5 1.8 %collective-permute-done.24.refs_2_ = bf16[16,2560]{1,0:T(8,128)(2,1)S(1)} collective-permute-done((bf16[16,2560]{1,0:T(8,128)(2,1)S(1)}, bf16[16,2560]{1,0:T(8,128)(2,1)S(1)}, u32[]{:S(2)}, u32[]{:S(2)}) %collective-permute-start.24) | collective-permute-done | bytes 81952 | tf_op jit(solution)/shard_map/cond/branch_3_fun/ppermute | solution.py:426
  22.3 0.0 collective-permute-done.23.refs_1_
  22.3 0.7 %rows.7 = (bf16[8,2,2560]{2,1,0:T(2,128)(2,1)S(1)}, bf16[2,2816]{1,0:T(2,128)(2,1)S(1)}, bf16[2,2816]{1,0:T(2,128)(2,1)S(1)}) custom-call(s32[4,4]{1,0:T(4,128)S(1)} %copy-done.11, s32[4,8]{1,0:T(4,128)S(1)} %copy-done.15, bf16[16,256]{1,0:T(8,128)(2,1)S(1)} %get-tuple-element.153.new_rows, bf16[16,2560]{1,0:T(8,128)(2,1)S(1)} %get-tuple-element.154.refs_0_, ...), custom_call_target="tpu_custom_call" | custom-call | tf_op jit(solution)/shard_map/cond/branch_3_fun/rows/pallas_call | solution.py:428
  23.0 2.0 %collective-permute-start.26 = (bf16[2,2816]{1,0:T(2,128)(2,1)S(1)}, bf16[2,2816]{1,0:T(2,128)(2,1)}, u32[]{:S(2)}, u32[]{:S(2)}) collective-permute-start(bf16[2,2816]{1,0:T(2,128)(2,1)S(1)} %get-tuple-element.155), channel_id=1, source_target_pairs={{8,0},{12,4},{0,8},{4,12},{9,1},{13,5},{1,9},{5,13},{10,2},{14,6},... | collective-permute-start | bytes 33800 | tf_op jit(solution)/shard_map/cond/branch_3_fun/ppermute | solution.py:437
  25.0 0.9 %collective-permute-start.27 = (bf16[2,2816]{1,0:T(2,128)(2,1)S(1)}, bf16[2,2816]{1,0:T(2,128)(2,1)}, u32[]{:S(2)}, u32[]{:S(2)}) collective-permute-start(bf16[2,2816]{1,0:T(2,128)(2,1)S(1)} %get-tuple-element.156), channel_id=1, source_target_pairs={{8,4},{12,0},{4,8},{0,12},{9,5},{13,1},{5,9},{1,13},{10,6},{14,2},... | collective-permute-start | bytes 33800 | tf_op jit(solution)/shard_map/cond/branch_3_fun/ppermute | solution.py:437
  25.9 6.3 %collective-permute-done.26 = bf16[2,2816]{1,0:T(2,128)(2,1)} collective-permute-done((bf16[2,2816]{1,0:T(2,128)(2,1)S(1)}, bf16[2,2816]{1,0:T(2,128)(2,1)}, u32[]{:S(2)}, u32[]{:S(2)}) %collective-permute-start.26) | collective-permute-done | bytes 11296 | tf_op jit(solution)/shard_map/cond/branch_3_fun/ppermute | solution.py:437
  32.2 0.0 collective-permute-done.27
  32.2 0.0 collective-permute-done.21
  32.2 0.0 collective-permute-done.22
  32.4 2.9 %place.1 = (bf16[8,2,2560]{2,1,0:T(2,128)(2,1)}, bf16[32,128,128]{2,1,0:T(8,128)(2,1)}, bf16[32,128,128]{2,1,0:T(8,128)(2,1)}) custom-call(s32[4,4]{1,0:T(4,128)} %mig.1, s32[4,8]{1,0:T(4,128)} %lens.1, s32[1,4,8]{2,1,0:T(4,128)} %bitcast.21, bf16[8,128,128]{2,1,0:T(8,128)(2,1)} %get-tuple-element.173.refs_0_, ...), custom_call_target="tpu_custom_call", output_to_operand_aliasing={{1}: (8, {}), {2}: (9, {})} | custom-call | tf_op jit(solution)/shard_map/place/pallas_call | solution.py:495
Async XLA Ops:
  2.8 6.4 %copy-start.3 = (bf16[32,128,128]{2,1,0:T(8,128)(2,1)S(1)}, bf16[32,128,128]{2,1,0:T(8,128)(2,1)}, u32[]{:S(2)}) copy-start(bf16[32,128,128]{2,1,0:T(8,128)(2,1)} %get-tuple-element.142.key_pool.kp) | copy-start | bytes 3145732 | tf_op jit(solution)/shard_map/cond
  2.8 6.4 %copy-start.7 = (bf16[32,128,128]{2,1,0:T(8,128)(2,1)S(1)}, bf16[32,128,128]{2,1,0:T(8,128)(2,1)}, u32[]{:S(2)}) copy-start(bf16[32,128,128]{2,1,0:T(8,128)(2,1)} %get-tuple-element.143.value_pool.vp) | copy-start | bytes 3145732 | tf_op jit(solution)/shard_map/cond
  2.8 6.4 %copy-start.11 = (s32[4,4]{1,0:T(4,128)S(1)}, s32[4,4]{1,0:T(4,128)}, u32[]{:S(2)}) copy-start(s32[4,4]{1,0:T(4,128)} %get-tuple-element.140.mig) | copy-start | bytes 196 | tf_op jit(solution)/shard_map/cond
  2.9 6.3 %copy-start.15 = (s32[4,8]{1,0:T(4,128)S(1)}, s32[4,8]{1,0:T(4,128)}, u32[]{:S(2)}) copy-start(s32[4,8]{1,0:T(4,128)} %get-tuple-element.146.lens) | copy-start | bytes 388 | tf_op jit(solution)/shard_map/cond
  2.9 6.3 %copy-start.19 = (s32[1,4,8]{2,1,0:T(4,128)S(1)}, s32[1,4,8]{2,1,0:T(4,128)}, u32[]{:S(2)}) copy-start(s32[1,4,8]{2,1,0:T(4,128)} %get-tuple-element.141.table) | copy-start | bytes 388 | tf_op jit(solution)/shard_map/cond
  4.5 27.7 %collective-permute-start.21 = (bf16[8,128,128]{2,1,0:T(8,128)(2,1)S(1)}, bf16[8,128,128]{2,1,0:T(8,128)(2,1)}, u32[]{:S(2)}, u32[]{:S(2)}) collective-permute-start(bf16[8,128,128]{2,1,0:T(8,128)(2,1)S(1)} %get-tuple-element.144), channel_id=1, source_target_pairs={{8,0},{12,4},{0,8},{4,12},{9,1},{13,5},{1,9},{5,13},{10,2},{14,6},... | collective-permute-start | bytes 786440 | tf_op jit(solution)/shard_map/cond/branch_3_fun/ppermute | solution.py:384
  8.1 24.1 %collective-permute-start.22 = (bf16[8,128,128]{2,1,0:T(8,128)(2,1)S(1)}, bf16[8,128,128]{2,1,0:T(8,128)(2,1)}, u32[]{:S(2)}, u32[]{:S(2)}) collective-permute-start(bf16[8,128,128]{2,1,0:T(8,128)(2,1)S(1)} %get-tuple-element.145), channel_id=1, source_target_pairs={{8,4},{12,0},{4,8},{0,12},{9,5},{13,1},{5,9},{1,13},{10,6},{14,2},... | collective-permute-start | bytes 786440 | tf_op jit(solution)/shard_map/cond/branch_3_fun/ppermute | solution.py:384
  15.7 4.8 %collective-permute-start.25 = (bf16[16,2560]{1,0:T(8,128)(2,1)S(1)}, bf16[16,2560]{1,0:T(8,128)(2,1)S(1)}, u32[]{:S(2)}, u32[]{:S(2)}) collective-permute-start(bf16[16,2560]{1,0:T(8,128)(2,1)S(1)} %get-tuple-element.154.refs_0_), channel_id=1, source_target_pairs={{0,3},{1,2},{2,1},{3,0},{4,7},{5,6},{6,5},{7,4},{8,11},{9,10},{10,... | collective-permute-start | bytes 245768 | tf_op jit(solution)/shard_map/cond/branch_3_fun/ppermute | solution.py:426
  16.4 5.8 %collective-permute-start.24 = (bf16[16,2560]{1,0:T(8,128)(2,1)S(1)}, bf16[16,2560]{1,0:T(8,128)(2,1)S(1)}, u32[]{:S(2)}, u32[]{:S(2)}) collective-permute-start(bf16[16,2560]{1,0:T(8,128)(2,1)S(1)} %get-tuple-element.154.refs_0_), channel_id=1, source_target_pairs={{0,2},{1,3},{2,0},{3,1},{4,6},{5,7},{6,4},{7,5},{8,10},{9,11},{10,... | collective-permute-start | bytes 245768 | tf_op jit(solution)/shard_map/cond/branch_3_fun/ppermute | solution.py:426
  17.3 4.9 %collective-permute-start.23 = (bf16[16,2560]{1,0:T(8,128)(2,1)S(1)}, bf16[16,2560]{1,0:T(8,128)(2,1)S(1)}, u32[]{:S(2)}, u32[]{:S(2)}) collective-permute-start(bf16[16,2560]{1,0:T(8,128)(2,1)S(1)} %get-tuple-element.154.refs_0_), channel_id=1, source_target_pairs={{0,1},{1,0},{2,3},{3,2},{4,5},{5,4},{6,7},{7,6},{8,9},{9,8},{10,11... | collective-permute-start | bytes 245768 | tf_op jit(solution)/shard_map/cond/branch_3_fun/ppermute | solution.py:426
  23.0 9.2 %collective-permute-start.26 = (bf16[2,2816]{1,0:T(2,128)(2,1)S(1)}, bf16[2,2816]{1,0:T(2,128)(2,1)}, u32[]{:S(2)}, u32[]{:S(2)}) collective-permute-start(bf16[2,2816]{1,0:T(2,128)(2,1)S(1)} %get-tuple-element.155), channel_id=1, source_target_pairs={{8,0},{12,4},{0,8},{4,12},{9,1},{13,5},{1,9},{5,13},{10,2},{14,6},... | collective-permute-start | bytes 33800 | tf_op jit(solution)/shard_map/cond/branch_3_fun/ppermute | solution.py:437
  25.0 7.2 %collective-permute-start.27 = (bf16[2,2816]{1,0:T(2,128)(2,1)S(1)}, bf16[2,2816]{1,0:T(2,128)(2,1)}, u32[]{:S(2)}, u32[]{:S(2)}) collective-permute-start(bf16[2,2816]{1,0:T(2,128)(2,1)S(1)} %get-tuple-element.156), channel_id=1, source_target_pairs={{8,4},{12,0},{4,8},{0,12},{9,5},{13,1},{5,9},{1,13},{10,6},{14,2},... | collective-permute-start | bytes 33800 | tf_op jit(solution)/shard_map/cond/branch_3_fun/ppermute | solution.py:437

commit v2 on v1

--- a/solution.py
+++ b/solution.py
@@ -70,7 +70,12 @@
                         do(load(n, which, p))
 
     each(lambda copy: copy.start())
-    token[0] = me
+    half = groups // 2
+    number = jnp.int32(0)
+    if half == 2:
+        for m in range(mig.shape[0]):
+            number = number | jnp.where(mig[m, 0] >= half, mig[m, 0] - half + 1, 0)
+    token[0] = number
     each(lambda copy: copy.wait())
 
 
@@ -348,6 +353,9 @@
 def run(
     near_hops,
     far_hops,
+    near,
+    far,
+    token,
     table,
     token_states,
     query_rows,
@@ -368,19 +376,8 @@
     heads = query_rows.shape[2] // head_dim
     pages = table.shape[1]
     pool_shape = jax.ShapeDtypeStruct(keys.shape, BF16)
-    moved_shape = jax.ShapeDtypeStruct((2 * pages, page_len, head_dim), BF16)
     limit = pltpu.CompilerParams(vmem_limit_bytes=63 * 2**20)
 
-    near, far, token = pl.pallas_call(
-        functools.partial(pack_kernel, groups),
-        out_shape=(moved_shape, moved_shape, jax.ShapeDtypeStruct((1,), jnp.int32)),
-        in_specs=[SMEM, SMEM, HBM, HBM],
-        out_specs=(VMEM, VMEM, SMEM),
-        scratch_shapes=[pltpu.SemaphoreType.DMA((2, 2, pages))],
-        compiler_params=pltpu.CompilerParams(vmem_limit_bytes=40 * 2**20),
-        cost_estimate=pl.CostEstimate(flops=0, bytes_accessed=1_000_000, transcendentals=0),
-        name="pack",
-    )(migrations, table, keys, values)
     pages_in = [lax.ppermute(near, "dec", near_hops)] + [lax.ppermute(far, "dec", hops) for hops in far_hops]
 
     key_mid, value_mid, partial, new_rows = pl.pallas_call(
@@ -441,9 +438,23 @@
 def moved(table, inputs):
     groups = lax.axis_size("dec")
     half = groups // 2
+    keys, values, _, migrations = inputs[-4:]
+    _, page_len, head_dim = keys.shape
+    pages = table.shape[1]
+    moved_shape = jax.ShapeDtypeStruct((2 * pages, page_len, head_dim), BF16)
+    near, far, token = pl.pallas_call(
+        functools.partial(pack_kernel, groups),
+        out_shape=(moved_shape, moved_shape, jax.ShapeDtypeStruct((1,), jnp.int32)),
+        in_specs=[SMEM, SMEM, HBM, HBM],
+        out_specs=(VMEM, VMEM, SMEM),
+        scratch_shapes=[pltpu.SemaphoreType.DMA((2, 2, pages))],
+        compiler_params=pltpu.CompilerParams(vmem_limit_bytes=40 * 2**20),
+        cost_estimate=pl.CostEstimate(flops=0, bytes_accessed=1_000_000, transcendentals=0),
+        name="pack",
+    )(migrations, table, keys, values)
     if half != 2:
-        return run(shifted(groups, half), (shifted(groups, 1), shifted(groups, 1 + half)), table, *inputs)
-    source_group = inputs[-1][:, 0]
+        far_hops = (shifted(groups, 1), shifted(groups, 1 + half))
+        return run(shifted(groups, half), far_hops, near, far, token, table, *inputs)
     branches = []
     for case in range(2**half):
         senders = [pair + half * (case >> pair & 1) for pair in range(half)]
@@ -453,9 +464,7 @@
         near_hops += [(b, a) for a, b in near_hops]
         far_hops += [(b, a) for a, b in far_hops]
         branches.append(functools.partial(run, near_hops, (far_hops,)))
-    bits = jnp.where(source_group >= half, source_group - half + 1, 0)
-    number = lax.reduce(bits, jnp.int32(0), lax.bitwise_or, (0,))
-    return lax.switch(number, branches, table, *inputs)
+    return lax.switch(token[0], branches, near, far, token, table, *inputs)
 
 
 def local(

time: 35.8 us -> 33.8 us (0.944)
  other arithmetic: 1.32 us -> 0 us
  loops' own time: 0.51 us -> 0.06 us
    another operation x1 -> x0, other arithmetic: 1.32 us -> none  [moved(): number = lax.reduce(bits, jnp.int32(0), lax.bitwise_or, (0,))]
    another operation x1, loops' own time: 0.51 us -> 0.06 us  [moved(): return lax.switch(token[0], branches, near, far, token, table, *inputs)]
  transfers between devices with their start and end apart: 7 -> 7, of which waited for: 3 -> 3; matrix products, arithmetic and copies ran while one was open for 0% -> 0% of each run, Pallas kernels for 20% -> 22%
where the time goes in v2:
time: 33.8 us; the launch traced here: 33.5 us
  Pallas kernels  11.7 us (35%)
  waiting for transfers between devices  10.9 us (32%)
  starting transfers between devices  9.52 us (28%)
  between operations  1.37 us (4%)
    pallas_call x1, Pallas kernels, run(): pl.pallas_call(functools.partial(attend_kernel, groups), out_shape=(pool_...  6.52 us
    ppermute x1, waiting for transfers between devices, run(): lax.ppermute(near_row, 'dec', near_hops)  6.26 us
    ppermute x3, waiting for transfers between devices, run(): lax.ppermute(partial, 'tp', [(i, i ^ n) for i in range(tp)])  4.64 us
    ppermute x1, starting transfers between devices, run(): lax.ppermute(near, 'dec', near_hops)  3.59 us
    pallas_call x1, Pallas kernels, local(): pl.pallas_call(functools.partial(place_kernel, groups, ways), out_shape=(...  2.78 us
    ppermute x1, starting transfers between devices, run(): lax.ppermute(near_row, 'dec', near_hops)  2.01 us
    ppermute x3, starting transfers between devices, run(): lax.ppermute(partial, 'tp', [(i, i ^ n) for i in range(tp)])  1.93 us
    pallas_call x1, Pallas kernels, moved(): pl.pallas_call(functools.partial(pack_kernel, groups), out_shape=(moved_s...  1.62 us
  transfers between devices with their start and end apart: 7, of which 3 were waited for; matrix products, arithmetic and copies ran while one was open for 0% of the time, Pallas kernels for 22%

profile of v2, /device:TPU:4, one launch (start us, length us, event | category | flops | bytes accessed | tf_op | source)
XLA Modules:
  0.0 33.5 jit_solution(17244413542266283899)
XLA Ops:
  0.6 0.0 copy-start.2
  0.6 0.0 copy-start.3
  0.7 0.0 copy-start.4
  0.7 0.0 copy-start.1
  0.7 0.0 copy-start
  0.7 1.6 %pack.1 = (bf16[8,128,128]{2,1,0:T(8,128)(2,1)S(1)}, bf16[8,128,128]{2,1,0:T(8,128)(2,1)S(1)}, s32[1]{0:T(128)}) custom-call(s32[4,4]{1,0:T(4,128)} %mig.3, s32[1,4,8]{2,1,0:T(4,128)} %bitcast.20, bf16[32,128,128]{2,1,0:T(8,128)(2,1)} %bitcast.10, bf16[32,128,128]{2,1,0:T(8,128)(2,1)} %bitcast.15), custom_call_target="tpu_custom_call" | custom-call | bytes 1000000 | tf_op jit(solution)/shard_map/pack/pallas_call | solution.py:445
  3.0 0.0 copy-done.2
  3.0 0.0 copy-done.3
  3.0 0.0 copy-done.4
  3.0 0.0 copy-done.1
  3.0 0.0 copy-done
  3.0 27.7 %conditional.1 = (bf16[8,128,128]{2,1,0:T(8,128)(2,1)}, bf16[8,128,128]{2,1,0:T(8,128)(2,1)}, bf16[2,2816]{1,0:T(2,128)(2,1)}, bf16[2,2816]{1,0:T(2,128)(2,1)}, ...) conditional(s32[]{:T(128)} %bitcast.3, ...), branch_computations={%region_0.0_spmd, %region_1.0_spmd, %region_2.0_spmd, %region_3.0_... | conditional | flops 1000000 | bytes 4170640 | solution.py:467
  3.0 3.6 %collective-permute-start.21 = (bf16[8,128,128]{2,1,0:T(8,128)(2,1)S(1)}, bf16[8,128,128]{2,1,0:T(8,128)(2,1)}, u32[]{:S(2)}, u32[]{:S(2)}) collective-permute-start(bf16[8,128,128]{2,1,0:T(8,128)(2,1)S(1)} %get-tuple-element.164), channel_id=1, source_target_pairs={{8,0},{12,4},{0,8},{4,12},{9,1},{13,5},{1,9},{5,13},{10,2},{14,6},... | collective-permute-start | bytes 786440 | tf_op jit(solution)/shard_map/cond/branch_3_fun/ppermute | solution.py:381
  6.6 1.1 %collective-permute-start.22 = (bf16[8,128,128]{2,1,0:T(8,128)(2,1)S(1)}, bf16[8,128,128]{2,1,0:T(8,128)(2,1)}, u32[]{:S(2)}, u32[]{:S(2)}) collective-permute-start(bf16[8,128,128]{2,1,0:T(8,128)(2,1)S(1)} %get-tuple-element.165), channel_id=1, source_target_pairs={{8,4},{12,0},{4,8},{0,12},{9,5},{13,1},{5,9},{1,13},{10,6},{14,2},... | collective-permute-start | bytes 786440 | tf_op jit(solution)/shard_map/cond/branch_3_fun/ppermute | solution.py:381
  7.7 6.5 %attend.7 = (bf16[32,128,128]{2,1,0:T(8,128)(2,1)}, bf16[32,128,128]{2,1,0:T(8,128)(2,1)}, bf16[16,2560]{1,0:T(8,128)(2,1)S(1)}, bf16[16,256]{1,0:T(8,128)(2,1)S(1)}) custom-call(s32[1]{0:T(128)} %get-tuple-element.168.token, s32[4,4]{1,0:T(4,128)S(1)} %get-tuple-element.166.mig, s32[4,8]{1,0:T(4,128)S(1)} %get-tuple-element.167.lens, ...), custom_call_target="tpu_custom_call" | custom-call | flops 1000000 | bytes 1000000 | tf_op jit(solution)/shard_map/cond/branch_3_fun/attend/pallas_call | solution.py:383
  14.2 0.7 %collective-permute-start.25 = (bf16[16,2560]{1,0:T(8,128)(2,1)S(1)}, bf16[16,2560]{1,0:T(8,128)(2,1)S(1)}, u32[]{:S(2)}, u32[]{:S(2)}) collective-permute-start(bf16[16,2560]{1,0:T(8,128)(2,1)S(1)} %get-tuple-element.178.refs_0_), channel_id=1, source_target_pairs={{0,3},{1,2},{2,1},{3,0},{4,7},{5,6},{6,5},{7,4},{8,11},{9,10},{10,... | collective-permute-start | bytes 245768 | tf_op jit(solution)/shard_map/cond/branch_3_fun/ppermute | solution.py:423
  15.0 0.9 %collective-permute-start.24 = (bf16[16,2560]{1,0:T(8,128)(2,1)S(1)}, bf16[16,2560]{1,0:T(8,128)(2,1)S(1)}, u32[]{:S(2)}, u32[]{:S(2)}) collective-permute-start(bf16[16,2560]{1,0:T(8,128)(2,1)S(1)} %get-tuple-element.178.refs_0_), channel_id=1, source_target_pairs={{0,2},{1,3},{2,0},{3,1},{4,6},{5,7},{6,4},{7,5},{8,10},{9,11},{10,... | collective-permute-start | bytes 245768 | tf_op jit(solution)/shard_map/cond/branch_3_fun/ppermute | solution.py:423
  15.9 0.3 collective-permute-start.23
  16.2 2.8 %collective-permute-done.25.refs_3_ = bf16[16,2560]{1,0:T(8,128)(2,1)S(1)} collective-permute-done((bf16[16,2560]{1,0:T(8,128)(2,1)S(1)}, bf16[16,2560]{1,0:T(8,128)(2,1)S(1)}, u32[]{:S(2)}, u32[]{:S(2)}) %collective-permute-start.25) | collective-permute-done | bytes 81952 | tf_op jit(solution)/shard_map/cond/branch_3_fun/ppermute | solution.py:423
  19.0 1.8 %collective-permute-done.24.refs_2_ = bf16[16,2560]{1,0:T(8,128)(2,1)S(1)} collective-permute-done((bf16[16,2560]{1,0:T(8,128)(2,1)S(1)}, bf16[16,2560]{1,0:T(8,128)(2,1)S(1)}, u32[]{:S(2)}, u32[]{:S(2)}) %collective-permute-start.24) | collective-permute-done | bytes 81952 | tf_op jit(solution)/shard_map/cond/branch_3_fun/ppermute | solution.py:423
  20.8 0.0 collective-permute-done.23.refs_1_
  20.8 0.7 %rows.7 = (bf16[8,2,2560]{2,1,0:T(2,128)(2,1)S(1)}, bf16[2,2816]{1,0:T(2,128)(2,1)S(1)}, bf16[2,2816]{1,0:T(2,128)(2,1)S(1)}) custom-call(s32[4,4]{1,0:T(4,128)S(1)} %get-tuple-element.166.mig, s32[4,8]{1,0:T(4,128)S(1)} %get-tuple-element.167.lens, bf16[16,256]{1,0:T(8,128)(2,1)S(1)} %get-tuple-element.177.new_rows, ...), custom_call_target="tpu_custom_call" | custom-call | tf_op jit(solution)/shard_map/cond/branch_3_fun/rows/pallas_call | solution.py:425
  21.6 2.0 %collective-permute-start.26 = (bf16[2,2816]{1,0:T(2,128)(2,1)S(1)}, bf16[2,2816]{1,0:T(2,128)(2,1)}, u32[]{:S(2)}, u32[]{:S(2)}) collective-permute-start(bf16[2,2816]{1,0:T(2,128)(2,1)S(1)} %get-tuple-element.179), channel_id=1, source_target_pairs={{8,0},{12,4},{0,8},{4,12},{9,1},{13,5},{1,9},{5,13},{10,2},{14,6},... | collective-permute-start | bytes 33800 | tf_op jit(solution)/shard_map/cond/branch_3_fun/ppermute | solution.py:434
  23.6 0.9 %collective-permute-start.27 = (bf16[2,2816]{1,0:T(2,128)(2,1)S(1)}, bf16[2,2816]{1,0:T(2,128)(2,1)}, u32[]{:S(2)}, u32[]{:S(2)}) collective-permute-start(bf16[2,2816]{1,0:T(2,128)(2,1)S(1)} %get-tuple-element.180), channel_id=1, source_target_pairs={{8,4},{12,0},{4,8},{0,12},{9,5},{13,1},{5,9},{1,13},{10,6},{14,2},... | collective-permute-start | bytes 33800 | tf_op jit(solution)/shard_map/cond/branch_3_fun/ppermute | solution.py:434
  24.5 6.3 %collective-permute-done.26 = bf16[2,2816]{1,0:T(2,128)(2,1)} collective-permute-done((bf16[2,2816]{1,0:T(2,128)(2,1)S(1)}, bf16[2,2816]{1,0:T(2,128)(2,1)}, u32[]{:S(2)}, u32[]{:S(2)}) %collective-permute-start.26) | collective-permute-done | bytes 11296 | tf_op jit(solution)/shard_map/cond/branch_3_fun/ppermute | solution.py:434
  30.7 0.0 collective-permute-done.27
  30.7 0.0 collective-permute-done.21
  30.7 0.0 collective-permute-done.22
  30.8 2.8 %place.1 = (bf16[8,2,2560]{2,1,0:T(2,128)(2,1)}, bf16[32,128,128]{2,1,0:T(8,128)(2,1)}, bf16[32,128,128]{2,1,0:T(8,128)(2,1)}) custom-call(s32[4,4]{1,0:T(4,128)S(1)} %copy-done.2, s32[4,8]{1,0:T(4,128)S(1)} %copy-done.3, s32[1,4,8]{2,1,0:T(4,128)S(1)} %bitcast.25, ...), custom_call_target="tpu_custom_call", output_to_operand_aliasing={{1}: (8, {}), {2}: (9, {})} | custom-call | tf_op jit(solution)/shard_map/place/pallas_call | solution.py:504
Async XLA Ops:
  0.6 2.3 %copy-start.2 = (s32[4,4]{1,0:T(4,128)S(1)}, s32[4,4]{1,0:T(4,128)}, u32[]{:S(2)}) copy-start(s32[4,4]{1,0:T(4,128)} %mig.3) | copy-start | bytes 196
  0.6 2.3 %copy-start.3 = (s32[4,8]{1,0:T(4,128)S(1)}, s32[4,8]{1,0:T(4,128)}, u32[]{:S(2)}) copy-start(s32[4,8]{1,0:T(4,128)} %lens.1) | copy-start | bytes 388
  0.7 2.3 %copy-start.4 = (s32[1,8,4]{1,2,0:T(4,128)S(1)}, s32[1,8,4]{1,2,0:T(4,128)}, u32[]{:S(2)}) copy-start(s32[1,8,4]{1,2,0:T(4,128)} %param.22) | copy-start | bytes 388
  0.7 2.3 %copy-start.1 = (bf16[32,1,128,128]{3,2,1,0:T(8,128)(2,1)S(1)}, bf16[32,1,128,128]{3,2,1,0:T(8,128)(2,1)}, u32[]{:S(2)}) copy-start(bf16[32,1,128,128]{3,2,1,0:T(8,128)(2,1)} %param.20) | copy-start | bytes 3145732
  0.7 2.3 %copy-start = (bf16[32,1,128,128]{3,2,1,0:T(8,128)(2,1)S(1)}, bf16[32,1,128,128]{3,2,1,0:T(8,128)(2,1)}, u32[]{:S(2)}) copy-start(bf16[32,1,128,128]{3,2,1,0:T(8,128)(2,1)} %param.19) | copy-start | bytes 3145732
  3.0 27.7 %collective-permute-start.21 = (bf16[8,128,128]{2,1,0:T(8,128)(2,1)S(1)}, bf16[8,128,128]{2,1,0:T(8,128)(2,1)}, u32[]{:S(2)}, u32[]{:S(2)}) collective-permute-start(bf16[8,128,128]{2,1,0:T(8,128)(2,1)S(1)} %get-tuple-element.164), channel_id=1, source_target_pairs={{8,0},{12,4},{0,8},{4,12},{9,1},{13,5},{1,9},{5,13},{10,2},{14,6},... | collective-permute-start | bytes 786440 | tf_op jit(solution)/shard_map/cond/branch_3_fun/ppermute | solution.py:381
  6.6 24.1 %collective-permute-start.22 = (bf16[8,128,128]{2,1,0:T(8,128)(2,1)S(1)}, bf16[8,128,128]{2,1,0:T(8,128)(2,1)}, u32[]{:S(2)}, u32[]{:S(2)}) collective-permute-start(bf16[8,128,128]{2,1,0:T(8,128)(2,1)S(1)} %get-tuple-element.165), channel_id=1, source_target_pairs={{8,4},{12,0},{4,8},{0,12},{9,5},{13,1},{5,9},{1,13},{10,6},{14,2},... | collective-permute-start | bytes 786440 | tf_op jit(solution)/shard_map/cond/branch_3_fun/ppermute | solution.py:381
  14.2 4.8 %collective-permute-start.25 = (bf16[16,2560]{1,0:T(8,128)(2,1)S(1)}, bf16[16,2560]{1,0:T(8,128)(2,1)S(1)}, u32[]{:S(2)}, u32[]{:S(2)}) collective-permute-start(bf16[16,2560]{1,0:T(8,128)(2,1)S(1)} %get-tuple-element.178.refs_0_), channel_id=1, source_target_pairs={{0,3},{1,2},{2,1},{3,0},{4,7},{5,6},{6,5},{7,4},{8,11},{9,10},{10,... | collective-permute-start | bytes 245768 | tf_op jit(solution)/shard_map/cond/branch_3_fun/ppermute | solution.py:423
  15.0 5.8 %collective-permute-start.24 = (bf16[16,2560]{1,0:T(8,128)(2,1)S(1)}, bf16[16,2560]{1,0:T(8,128)(2,1)S(1)}, u32[]{:S(2)}, u32[]{:S(2)}) collective-permute-start(bf16[16,2560]{1,0:T(8,128)(2,1)S(1)} %get-tuple-element.178.refs_0_), channel_id=1, source_target_pairs={{0,2},{1,3},{2,0},{3,1},{4,6},{5,7},{6,4},{7,5},{8,10},{9,11},{10,... | collective-permute-start | bytes 245768 | tf_op jit(solution)/shard_map/cond/branch_3_fun/ppermute | solution.py:423
  15.9 4.9 %collective-permute-start.23 = (bf16[16,2560]{1,0:T(8,128)(2,1)S(1)}, bf16[16,2560]{1,0:T(8,128)(2,1)S(1)}, u32[]{:S(2)}, u32[]{:S(2)}) collective-permute-start(bf16[16,2560]{1,0:T(8,128)(2,1)S(1)} %get-tuple-element.178.refs_0_), channel_id=1, source_target_pairs={{0,1},{1,0},{2,3},{3,2},{4,5},{5,4},{6,7},{7,6},{8,9},{9,8},{10,11... | collective-permute-start | bytes 245768 | tf_op jit(solution)/shard_map/cond/branch_3_fun/ppermute | solution.py:423
  21.6 9.2 %collective-permute-start.26 = (bf16[2,2816]{1,0:T(2,128)(2,1)S(1)}, bf16[2,2816]{1,0:T(2,128)(2,1)}, u32[]{:S(2)}, u32[]{:S(2)}) collective-permute-start(bf16[2,2816]{1,0:T(2,128)(2,1)S(1)} %get-tuple-element.179), channel_id=1, source_target_pairs={{8,0},{12,4},{0,8},{4,12},{9,1},{13,5},{1,9},{5,13},{10,2},{14,6},... | collective-permute-start | bytes 33800 | tf_op jit(solution)/shard_map/cond/branch_3_fun/ppermute | solution.py:434
  23.6 7.2 %collective-permute-start.27 = (bf16[2,2816]{1,0:T(2,128)(2,1)S(1)}, bf16[2,2816]{1,0:T(2,128)(2,1)}, u32[]{:S(2)}, u32[]{:S(2)}) collective-permute-start(bf16[2,2816]{1,0:T(2,128)(2,1)S(1)} %get-tuple-element.180), channel_id=1, source_target_pairs={{8,4},{12,0},{4,8},{0,12},{9,5},{13,1},{5,9},{1,13},{10,6},{14,2},... | collective-permute-start | bytes 33800 | tf_op jit(solution)/shard_map/cond/branch_3_fun/ppermute | solution.py:434
